TPU v7x, 32 devices: a whole 2x2x4 slice. The times are simulated.
32 devices in a mesh: cd: 8 (over z, y), ab: 4 (over x, core).
Axes of the slice: x: 2, y: 2, z: 4, core: 2. Of those that a mesh axis runs over, the one named last changes fastest.
Arguments:
- amplitudes: bfloat16 [512, 8, 800], P('cd', None, 'ab'), may hold values from -6 to 6
- integrals: bfloat16 [8, 800, 2048], P('cd', None, 'ab'), may hold values from -0.078125 to 0.078125
Outputs:
- ladder: float32 [512, 2048], P('cd', 'ab')
All inputs are finite; a program needn't handle non-finite values.
Results may differ from a plain program's by a relative error of at most 0.0003.
Values may be sent and summed in bfloat16 or wider, within the bound.
A program may use at most 64 MiB of HBM per device.

v0:
```python
import jax
import jax.numpy as jnp
from jax import lax
from jax.sharding import PartitionSpec as P


def on_device(amplitudes, integrals):
    c_local, d_width, ab_local = integrals.shape
    assembled = lax.all_gather(amplitudes, "ab", axis=2, tiled=True)
    complete = lax.all_to_all(assembled, "cd", split_axis=1, concat_axis=0, tiled=True)
    flat = complete.reshape(complete.shape[0], c_local * d_width)
    slab = integrals.reshape(c_local * d_width, ab_local)
    return lax.psum_scatter(
        jnp.dot(flat, slab, preferred_element_type=jnp.float32),
        "cd",
        scatter_dimension=0,
        tiled=True,
    )


def solution(mesh):
    in_specs = (P("cd", None, "ab"), P("cd", None, "ab"))
    out_specs = P("cd", "ab")
    return jax.shard_map(
        on_device, mesh=mesh, in_specs=in_specs, out_specs=out_specs, check_vma=False
    )
```

profile of v0, /device:TPU:0, one launch (start us, length us, event | category | flops | bytes accessed | tf_op | source)
XLA Modules:
  0.0 125.0 jit_solution(4527043416997278588)
XLA Ops:
  6.5 0.0 copy-start
  6.5 0.0 reduce-scatter.2.cloned.1.call-start
  6.5 1.4 %copy.4 = bf16[64,8,200]{0,1,2:T(8,128)(2,1)S(1)} copy(bf16[64,8,200]{2,1,0:T(8,128)(2,1)} %param.2) | data formatting | bytes 409600 | tf_op args[0]
  8.0 14.7 %all_gather.3 = bf16[64,8,800]{0,1,2:T(8,128)(2,1)S(1)} all-gather(bf16[64,8,200]{0,1,2:T(8,128)(2,1)S(1)} %copy.4), channel_id=1, replica_groups=mesh['cd'=8,'ab'=4] {'ab'}, dimensions={2}, use_global_device_ids=true | all-gather | bytes 1024000 | tf_op jit(solution)/shard_map/all_gather | solution.py:9
  22.6 1.9 %copy.5 = bf16[64,8,800]{2,0,1:T(8,128)(2,1)S(1)} copy(bf16[64,8,800]{0,1,2:T(8,128)(2,1)S(1)} %all_gather.3) | data formatting | bytes 1638400 | tf_op jit(solution)/shard_map/all_gather | solution.py:9
  24.6 29.4 %all_to_all.15 = bf16[64,8,800]{2,0,1:T(8,128)(2,1)S(1)} all-to-all(bf16[64,8,800]{2,0,1:T(8,128)(2,1)S(1)} %copy.5), channel_id=1, replica_groups=mesh['cd'=8,'ab'=4] {'cd'}, dimensions={1} | all-to-all | bytes 1638400 | tf_op jit(solution)/shard_map/all_to_all | solution.py:10
  54.0 0.0 copy-done
  54.0 1.7 %fusion = f32[512,512]{1,0:T(8,128)} fusion(bf16[512,800]{1,0:T(8,128)(2,1)S(1)} %bitcast.9, bf16[1,800,512]{2,1,0:T(8,128)(2,1)S(1)} %copy-done), kind=kOutput, calls=%fused_computation | convolution fusion | flops 419430400 | bytes 2686976 | tf_op jit(solution)/shard_map/dot_general | solution.py:14
  55.7 0.0 reduce-scatter.2.cloned.1.call-update
  55.7 62.4 %reduce-scatter.2.cloned.1.call-done = f32[64,512]{1,0:T(8,128)} async-done(((f32[512,512]{1,0:T(8,128)}), f32[64,512]{1,0:T(8,128)}) %reduce-scatter.2.cloned.1.call-update) | async-done | bytes 131088 | tf_op jit(solution)/shard_map/reduce_scatter | solution.py:13
Async XLA Ops:
  6.5 47.5 %copy-start = (bf16[1,800,512]{2,1,0:T(8,128)(2,1)S(1)}, bf16[1,800,512]{2,1,0:T(8,128)(2,1)}, u32[]{:S(2)}) copy-start(bf16[1,800,512]{2,1,0:T(8,128)(2,1)} %param.3) | copy-start | bytes 2457604
  6.5 111.6 %reduce-scatter.2.cloned.1.call-start = ((), (), s32[]{:S(2)}) async-start(), calls=%async_computation.2 | async-start | bytes 1179648 | tf_op jit(solution)/shard_map/reduce_scatter | solution.py:13
Sparse Core Ops, SparseCore 0:
  55.8 62.2 reduce-scatter.1
where the time goes:
time: 125 us
  waiting for transfers between devices  62.4 us (50%)
  blocking collectives  44.1 us (35%)
  between operations  13.4 us (11%)
  local copies, waits for them, and re-layouts  3.34 us (3%)
  matrix products  1.68 us (1%)
    reduce_scatter x1, waiting for transfers between devices, on_device(): lax.psum_scatter(jnp.dot(flat, slab, preferred_element_type=jnp.float32),...  62.4 us
    all_to_all x1, blocking collectives, on_device(): lax.all_to_all(assembled, 'cd', split_axis=1, concat_axis=0, tiled=True)  29.4 us
    all_gather x1, blocking collectives, on_device(): assembled = lax.all_gather(amplitudes, 'ab', axis=2, tiled=True)  14.7 us
  transfers between devices with their start and end apart: 1, of which 1 were waited for; matrix products, arithmetic and copies ran while one was open for 0% of the time, Pallas kernels for 0%

commit v1 on v0

v1 whole, which is shorter than its diff:
```python
import functools

import jax
import jax.numpy as jnp
from jax import lax
from jax.experimental import pallas as pl
from jax.experimental.pallas import tpu as pltpu
from jax.sharding import PartitionSpec as P

MESH = pl.DeviceIdType.MESH
LANES = 128
ORDER = (7, 5, 6, 3, 4, 1, 2, 0)


def flip(index, bits):
    out = index
    bit = 1
    while bit <= bits:
        if bits & bit:
            out = out + bit - 2 * bit * (lax.div(index, bit) % 2)
        bit *= 2
    return out


def kernel(
    amp_ref, int_ref, out_ref, stage, held, slab, ysend, yrecv, zsum, zrecv,
    a2a_s, a2a_r, xf_s, xf_r, cf_s, cf_r, y_s, y_r, z_s, z_r, local_sem,
):
    cd = lax.axis_index("cd")
    ab = lax.axis_index("ab")
    rows, n_cd, width = amp_ref.shape
    wide = stage.shape[2]
    n_ab = slab.shape[0]
    columns = int_ref.shape[1]
    half = n_cd // 2

    peers = [(flip(cd, k), ab) for k in range(1, n_cd)]
    peers += [(cd, flip(ab, 1)), (cd, flip(ab, 2))]
    barrier = pltpu.get_barrier_semaphore()
    for peer in peers:
        pl.semaphore_signal(barrier, inc=1, device_id=peer, device_id_type=MESH)

    stage[:, :, width:] = jnp.zeros((n_cd, rows, wide - width), stage.dtype)
    for c in range(n_cd):
        stage[c, :, :width] = amp_ref[:, c, :]

    pl.semaphore_wait(barrier, len(peers))

    def remote(src, dst, s, r, peer):
        return pltpu.make_async_remote_copy(
            src_ref=src, dst_ref=dst, send_sem=s, recv_sem=r,
            device_id=peer, device_id_type=MESH,
        )

    a2a = {}
    for k in ORDER:
        if k:
            a2a[k] = remote(stage.at[flip(cd, k)], held.at[0, k], a2a_s.at[k], a2a_r.at[k], (flip(cd, k), ab))
            a2a[k].start()
    own = pltpu.make_async_copy(stage.at[cd], held.at[0, 0], local_sem)
    own.start()

    for j in range(n_ab):
        slab[j, :width, :] = int_ref[j * width : (j + 1) * width, :]
        slab[j, width:, :] = jnp.zeros((wide - width, columns), slab.dtype)

    xf = {k: remote(held.at[0, k], held.at[2, k], xf_s.at[k], xf_r.at[k], (cd, flip(ab, 2))) for k in ORDER}
    cf = {
        (r, k): remote(held.at[r, k], held.at[r + 1, k], cf_s.at[r // 2, k], cf_r.at[r // 2, k], (cd, flip(ab, 1)))
        for k in ORDER
        for r in (0, 2)
    }
    ycopy = {
        h: remote(ysend.at[h], yrecv.at[h], y_s.at[h], y_r.at[h], (flip(cd, 1), ab)) for h in range(half)
    }
    zcopy = {
        h: remote(zsum.at[h], zrecv.at[h], z_s.at[h], z_r.at[h], (flip(cd, 2 * h), ab)) for h in range(1, half)
    }

    def arrive(k):
        (a2a[k].wait_recv if k else own.wait)()
        xf[k].start()
        cf[0, k].start()

    def relay(k):
        xf[k].wait_recv()
        cf[2, k].start()

    def product(k):
        cf[0, k].wait_recv()
        cf[2, k].wait_recv()
        total = jnp.dot(held[0, k], slab[ab], preferred_element_type=jnp.float32)
        for r in range(1, n_ab):
            total += jnp.dot(held[r, k], slab[flip(ab, r)], preferred_element_type=jnp.float32)
        if k % 2:
            ysend[k // 2] = total
            ycopy[k // 2].start()
        else:
            zsum[k // 2] = total

    def collect(h):
        ycopy[h].wait_recv()
        zsum[h] += yrecv[h]
        if h:
            zcopy[h].start()

    after = {6: 3, 4: 2}
    for step, k in enumerate(ORDER):
        arrive(k)
        if step >= 1:
            relay(ORDER[step - 1])
        if step >= 2:
            product(ORDER[step - 2])
        if step >= 3 and ORDER[step - 3] in after:
            collect(after[ORDER[step - 3]])
    relay(ORDER[-1])
    product(ORDER[-2])
    collect(1)
    product(ORDER[-1])
    collect(0)
    total = zsum[0]
    for h in range(half - 1, 0, -1):
        zcopy[h].wait_recv()
        total += zrecv[h]
    out_ref[...] = total

    for k in ORDER:
        if k:
            a2a[k].wait_send()
        xf[k].wait_send()
        cf[0, k].wait_send()
        cf[2, k].wait_send()
    for h in range(half):
        ycopy[h].wait_send()
        if h:
            zcopy[h].wait_send()


def by_kernel(amplitudes, integrals, n_ab):
    rows, n_cd, width = amplitudes.shape
    columns = integrals.shape[2]
    wide = -(-width // LANES) * LANES
    half = n_cd // 2
    dma = pltpu.SemaphoreType.DMA
    block = pltpu.VMEM((half, rows, columns), jnp.float32)
    return pl.pallas_call(
        kernel,
        out_shape=jax.ShapeDtypeStruct((rows, columns), jnp.float32),
        in_specs=[pl.BlockSpec(memory_space=pltpu.VMEM)] * 2,
        out_specs=pl.BlockSpec(memory_space=pltpu.VMEM),
        scratch_shapes=[
            pltpu.VMEM((n_cd, rows, wide), amplitudes.dtype),
            pltpu.VMEM((n_ab, n_cd, rows, wide), amplitudes.dtype),
            pltpu.VMEM((n_ab, wide, columns), integrals.dtype),
            block, block, block, block,
            dma((n_cd,)), dma((n_cd,)), dma((n_cd,)), dma((n_cd,)),
            dma((2, n_cd)), dma((2, n_cd)),
            dma((half,)), dma((half,)), dma((half,)), dma((half,)),
            dma,
        ],
        compiler_params=pltpu.CompilerParams(
            collective_id=0, has_side_effects=True, vmem_limit_bytes=32 * 1024 * 1024
        ),
    )(amplitudes, integrals.reshape(integrals.shape[1], columns))


def by_collectives(amplitudes, integrals):
    c_local, depth, columns = integrals.shape
    mine = lax.all_to_all(amplitudes, "cd", split_axis=1, concat_axis=0, tiled=True)
    complete = lax.all_gather(mine, "ab", axis=2, tiled=True)
    flat = complete.reshape(complete.shape[0], c_local * depth)
    slab = integrals.reshape(c_local * depth, columns)
    partial = jnp.dot(flat, slab, preferred_element_type=jnp.float32)
    return lax.psum_scatter(partial, "cd", scatter_dimension=0, tiled=True)


def on_device(n_cd, n_ab, amplitudes, integrals):
    rows = amplitudes.shape[0]
    if n_cd == 8 and n_ab == 4 and integrals.shape[0] == 1 and rows % 16 == 0:
        return by_kernel(amplitudes, integrals, n_ab)
    return by_collectives(amplitudes, integrals)


def solution(mesh):
    specs = (P("cd", None, "ab"), P("cd", None, "ab"))
    return jax.shard_map(
        functools.partial(on_device, mesh.shape["cd"], mesh.shape["ab"]),
        mesh=mesh, in_specs=specs, out_specs=P("cd", "ab"), check_vma=False,
    )
```

time: 125 us -> 37.7 us (0.30)
  waiting for transfers between devices: 62.4 us -> 0 us
  blocking collectives: 44.1 us -> 0 us
  Pallas kernels: 0 us -> 34.8 us
  between operations: 13.4 us -> 0.01 us
  matrix products: 1.68 us -> 0 us
    reduce_scatter x1 -> x0, waiting for transfers between devices: 62.4 us -> none  [on_device(): lax.psum_scatter(jnp.dot(flat, slab, preferred_element_type=jnp.float32),...]
    pallas_call x0 -> x1, Pallas kernels: none -> 34.8 us  [by_kernel(): pl.pallas_call(kernel, out_shape=jax.ShapeDtypeStruct((rows, columns), jn...]
    all_to_all x1 -> x0, blocking collectives: 29.4 us -> none  [on_device(): lax.all_to_all(assembled, 'cd', split_axis=1, concat_axis=0, tiled=True)]
    all_gather x1 -> x0, blocking collectives: 14.7 us -> none  [on_device(): assembled = lax.all_gather(amplitudes, 'ab', axis=2, tiled=True)]
    all_gather x1 -> x0, local copies, waits for them, and re-layouts: 1.93 us -> none  [on_device(): assembled = lax.all_gather(amplitudes, 'ab', axis=2, tiled=True)]
    dot_general x1 -> x0, matrix products: 1.68 us -> none  [on_device(): jnp.dot(flat, slab, preferred_element_type=jnp.float32)]
    unnamed x3 -> x5, local copies, waits for them, and re-layouts: 1.41 us -> 2.75 us
  transfers between devices with their start and end apart: 1 -> 0, of which waited for: 1 -> 0; matrix products, arithmetic and copies ran while one was open for 0% -> 0% of each run, Pallas kernels for 0% -> 0%
where the time goes in v1:
time: 37.7 us; the launch traced here: 37.5 us
  Pallas kernels  34.8 us (92%)
  local copies, waits for them, and re-layouts  2.75 us (7%)
    pallas_call x1, Pallas kernels, by_kernel(): pl.pallas_call(kernel, out_shape=jax.ShapeDtypeStruct((rows, columns), jn...  34.8 us
    unnamed x5, local copies, waits for them, and re-layouts  2.75 us

profile of v1, /device:TPU:0, one launch (start us, length us, event | category | flops | bytes accessed | tf_op | source)
XLA Modules:
  0.0 37.5 jit_solution(17208675909266775131)
XLA Ops:
  0.0 0.0 copy-start
  0.0 1.1 %copy-done = bf16[1,800,512]{2,1,0:T(8,128)(2,1)S(1)} copy-done((bf16[1,800,512]{2,1,0:T(8,128)(2,1)S(1)}, bf16[1,800,512]{2,1,0:T(8,128)(2,1)}, u32[]{:S(2)}) %copy-start) | copy-done | bytes 819224
  1.1 0.0 copy-start.1
  1.1 0.9 %copy-done.1 = bf16[64,8,200]{2,1,0:T(8,128)(2,1)S(1)} copy-done((bf16[64,8,200]{2,1,0:T(8,128)(2,1)S(1)}, bf16[64,8,200]{2,1,0:T(8,128)(2,1)}, u32[]{:S(2)}) %copy-start.1) | copy-done | bytes 204824
  2.1 34.8 %shard_map.28 = f32[64,512]{1,0:T(8,128)S(1)} custom-call(bf16[64,8,200]{2,1,0:T(8,128)(2,1)S(1)} %copy-done.1, bf16[800,512]{1,0:T(8,128)(2,1)S(1)} %bitcast.1), custom_call_target="tpu_custom_call" | custom-call | tf_op jit(solution)/shard_map/pallas_call | solution.py:146
  36.9 0.7 %copy.4 = f32[64,512]{1,0:T(8,128)} copy(f32[64,512]{1,0:T(8,128)S(1)} %shard_map.28) | data formatting | bytes 262144
Async XLA Ops:
  0.0 1.1 %copy-start = (bf16[1,800,512]{2,1,0:T(8,128)(2,1)S(1)}, bf16[1,800,512]{2,1,0:T(8,128)(2,1)}, u32[]{:S(2)}) copy-start(bf16[1,800,512]{2,1,0:T(8,128)(2,1)} %param.3) | copy-start | bytes 2457604
  1.1 0.9 %copy-start.1 = (bf16[64,8,200]{2,1,0:T(8,128)(2,1)S(1)}, bf16[64,8,200]{2,1,0:T(8,128)(2,1)}, u32[]{:S(2)}) copy-start(bf16[64,8,200]{2,1,0:T(8,128)(2,1)} %amp_ref.1) | copy-start | bytes 614404

commit v2 on v1

--- a/solution.py
+++ b/solution.py
@@ -9,7 +9,14 @@
 
 MESH = pl.DeviceIdType.MESH
 LANES = 128
-ORDER = (7, 5, 6, 3, 4, 1, 2, 0)
+ORDER = (5, 7, 3, 1, 4, 6, 2, 0)
+DIRECT = ()
+PLAN = (
+    ("a", 5), ("r", 5), ("a", 7), ("p", 5), ("a", 3), ("a", 1), ("r", 7), ("p", 7),
+    ("a", 4), ("a", 6), ("a", 2), ("r", 3), ("p", 3), ("r", 1), ("p", 1),
+    ("r", 4), ("p", 4), ("s", 2), ("r", 6), ("p", 6), ("s", 3),
+    ("r", 2), ("p", 2), ("s", 1), ("r", 0), ("p", 0), ("s", 0),
+)
 
 
 def flip(index, bits):
@@ -24,7 +31,7 @@
 
 def kernel(
     amp_ref, int_ref, out_ref, stage, held, slab, ysend, yrecv, zsum, zrecv,
-    a2a_s, a2a_r, xf_s, xf_r, cf_s, cf_r, y_s, y_r, z_s, z_r, local_sem,
+    amp, whole, a2a_s, a2a_r, xf_s, xf_r, cf_s, cf_r, y_s, y_r, z_s, z_r, local_sem,
 ):
     cd = lax.axis_index("cd")
     ab = lax.axis_index("ab")
@@ -34,15 +41,21 @@
     columns = int_ref.shape[1]
     half = n_cd // 2
 
+    load_amp = pltpu.make_async_copy(amp_ref, amp, local_sem.at[0])
+    load_int = pltpu.make_async_copy(int_ref, whole, local_sem.at[1])
+    load_amp.start()
+    load_int.start()
     peers = [(flip(cd, k), ab) for k in range(1, n_cd)]
     peers += [(cd, flip(ab, 1)), (cd, flip(ab, 2))]
+    peers += [(flip(cd, k), flip(ab, 2)) for k in DIRECT]
     barrier = pltpu.get_barrier_semaphore()
     for peer in peers:
         pl.semaphore_signal(barrier, inc=1, device_id=peer, device_id_type=MESH)
 
     stage[:, :, width:] = jnp.zeros((n_cd, rows, wide - width), stage.dtype)
+    load_amp.wait()
     for c in range(n_cd):
-        stage[c, :, :width] = amp_ref[:, c, :]
+        stage[c, :, :width] = amp[:, c, :]
 
     pl.semaphore_wait(barrier, len(peers))
 
@@ -52,24 +65,33 @@
             device_id=peer, device_id_type=MESH,
         )
 
-    a2a = {}
+    def block(r, k):
+        return held.at[r, k] if r or k else stage.at[cd]
+
+    a2a, xf = {}, {}
     for k in ORDER:
+        away = flip(cd, k)
         if k:
-            a2a[k] = remote(stage.at[flip(cd, k)], held.at[0, k], a2a_s.at[k], a2a_r.at[k], (flip(cd, k), ab))
+            a2a[k] = remote(stage.at[away], held.at[0, k], a2a_s.at[k], a2a_r.at[k], (away, ab))
             a2a[k].start()
-    own = pltpu.make_async_copy(stage.at[cd], held.at[0, 0], local_sem)
-    own.start()
-
-    for j in range(n_ab):
-        slab[j, :width, :] = int_ref[j * width : (j + 1) * width, :]
-        slab[j, width:, :] = jnp.zeros((wide - width, columns), slab.dtype)
-
-    xf = {k: remote(held.at[0, k], held.at[2, k], xf_s.at[k], xf_r.at[k], (cd, flip(ab, 2))) for k in ORDER}
+        if k in DIRECT:
+            xf[k] = remote(stage.at[away], held.at[2, k], xf_s.at[k], xf_r.at[k], (away, flip(ab, 2)))
+            xf[k].start()
+        else:
+            xf[k] = remote(block(0, k), held.at[2, k], xf_s.at[k], xf_r.at[k], (cd, flip(ab, 2)))
     cf = {
-        (r, k): remote(held.at[r, k], held.at[r + 1, k], cf_s.at[r // 2, k], cf_r.at[r // 2, k], (cd, flip(ab, 1)))
+        (r, k): remote(block(r, k), held.at[r + 1, k], cf_s.at[r // 2, k], cf_r.at[r // 2, k], (cd, flip(ab, 1)))
         for k in ORDER
         for r in (0, 2)
     }
+    xf[0].start()
+    cf[0, 0].start()
+
+    load_int.wait()
+    for j in range(n_ab):
+        slab[j, :width, :] = whole[j * width : (j + 1) * width, :]
+        slab[j, width:, :] = jnp.zeros((wide - width, columns), slab.dtype)
+
     ycopy = {
         h: remote(ysend.at[h], yrecv.at[h], y_s.at[h], y_r.at[h], (flip(cd, 1), ab)) for h in range(half)
     }
@@ -78,8 +100,9 @@
     }
 
     def arrive(k):
-        (a2a[k].wait_recv if k else own.wait)()
-        xf[k].start()
+        a2a[k].wait_recv()
+        if k not in DIRECT:
+            xf[k].start()
         cf[0, k].start()
 
     def relay(k):
@@ -89,7 +112,7 @@
     def product(k):
         cf[0, k].wait_recv()
         cf[2, k].wait_recv()
-        total = jnp.dot(held[0, k], slab[ab], preferred_element_type=jnp.float32)
+        total = jnp.dot(block(0, k)[...], slab[ab], preferred_element_type=jnp.float32)
         for r in range(1, n_ab):
             total += jnp.dot(held[r, k], slab[flip(ab, r)], preferred_element_type=jnp.float32)
         if k % 2:
@@ -104,22 +127,11 @@
         if h:
             zcopy[h].start()
 
-    after = {6: 3, 4: 2}
-    for step, k in enumerate(ORDER):
-        arrive(k)
-        if step >= 1:
-            relay(ORDER[step - 1])
-        if step >= 2:
-            product(ORDER[step - 2])
-        if step >= 3 and ORDER[step - 3] in after:
-            collect(after[ORDER[step - 3]])
-    relay(ORDER[-1])
-    product(ORDER[-2])
-    collect(1)
-    product(ORDER[-1])
-    collect(0)
+    act = {"a": arrive, "r": relay, "p": product, "s": collect}
+    for what, k in PLAN:
+        act[what](k)
     total = zsum[0]
-    for h in range(half - 1, 0, -1):
+    for h in (2, 3, 1):
         zcopy[h].wait_recv()
         total += zrecv[h]
     out_ref[...] = total
@@ -146,20 +158,22 @@
     return pl.pallas_call(
         kernel,
         out_shape=jax.ShapeDtypeStruct((rows, columns), jnp.float32),
-        in_specs=[pl.BlockSpec(memory_space=pltpu.VMEM)] * 2,
+        in_specs=[pl.BlockSpec(memory_space=pltpu.HBM)] * 2,
         out_specs=pl.BlockSpec(memory_space=pltpu.VMEM),
         scratch_shapes=[
             pltpu.VMEM((n_cd, rows, wide), amplitudes.dtype),
             pltpu.VMEM((n_ab, n_cd, rows, wide), amplitudes.dtype),
             pltpu.VMEM((n_ab, wide, columns), integrals.dtype),
             block, block, block, block,
+            pltpu.VMEM(amplitudes.shape, amplitudes.dtype),
+            pltpu.VMEM(integrals.shape[1:], integrals.dtype),
             dma((n_cd,)), dma((n_cd,)), dma((n_cd,)), dma((n_cd,)),
             dma((2, n_cd)), dma((2, n_cd)),
             dma((half,)), dma((half,)), dma((half,)), dma((half,)),
-            dma,
+            dma((2,)),
         ],
         compiler_params=pltpu.CompilerParams(
-            collective_id=0, has_side_effects=True, vmem_limit_bytes=32 * 1024 * 1024
+            collective_id=0, has_side_effects=True, vmem_limit_bytes=56 * 1024 * 1024
         ),
     )(amplitudes, integrals.reshape(integrals.shape[1], columns))
 

time: 37.7 us -> 35.7 us (0.947)
  local copies, waits for them, and re-layouts: 2.75 us -> 1.57 us
  Pallas kernels: 34.8 us -> 34 us
    unnamed x5 -> x1, local copies, waits for them, and re-layouts: 2.75 us -> 1.57 us
    pallas_call x1, Pallas kernels: 34.8 us -> 34 us  [by_kernel(): pl.pallas_call(kernel, out_shape=jax.ShapeDtypeStruct((rows, columns), jn...]
where the time goes in v2:
time: 35.7 us; the launch traced here: 35.5 us
  Pallas kernels  34 us (95%)
  local copies, waits for them, and re-layouts  1.57 us (4%)
    pallas_call x1, Pallas kernels, by_kernel(): pl.pallas_call(kernel, out_shape=jax.ShapeDtypeStruct((rows, columns), jn...  34 us
    unnamed x1, local copies, waits for them, and re-layouts  1.57 us

profile of v2, /device:TPU:0, one launch (start us, length us, event | category | flops | bytes accessed | tf_op | source)
XLA Modules:
  0.0 35.5 jit_solution(1037223946229334081)
XLA Ops:
  0.0 34.0 %shard_map.28 = f32[64,512]{1,0:T(8,128)} custom-call(bf16[64,8,200]{2,1,0:T(8,128)(2,1)} %amp_ref.1, bf16[800,512]{1,0:T(8,128)(2,1)} %bitcast.1), custom_call_target="tpu_custom_call" | custom-call | tf_op jit(solution)/shard_map/pallas_call | solution.py:158
  34.0 1.6 %copy.4 = f32[64,512]{1,0:T(8,128)} copy(f32[64,512]{1,0:T(8,128)} %shard_map.28) | data formatting | bytes 262144
